TPU v7x, 32 devices: a whole 2x2x4 slice. The times are simulated.
32 devices in a mesh: fsdp: 2 (over y), dp: 4 (over z), tensor: 4 (over x, core).
Axes of the slice: x: 2, y: 2, z: 4, core: 2. Of those that a mesh axis runs over, the one named last changes fastest.
Arguments:
- master_weight: float32 [4096, 14336], P(('fsdp', 'dp'), 'tensor'), may hold values from -0.09375 to 0.09375
- first_moment: bfloat16 [4096, 14336], P(('fsdp', 'dp'), 'tensor'), may hold values from -6 to 6
- second_moment: bfloat16 [4096, 14336], P(('fsdp', 'dp'), 'tensor'), may hold values from 0.25 to 16
- teacher_weight: float32 [4096, 14336], P(('fsdp', 'dp'), 'tensor'), may hold values from -0.09375 to 0.09375
- grad_parts: bfloat16 [4, 4096, 14336], P('dp', 'fsdp', 'tensor'), may hold values from -6 to 6
- embed_table: bfloat16 [4096, 64128], P(('fsdp', 'dp', 'tensor')), may hold values from -6 to 6
- token_ids: int32 [2, 256], P('fsdp'), may hold values from 0 to 64127
- pair_ids: int32 [2, 256], P('fsdp'), may hold values from 0 to 7, never falling along the last dimension, each value on 1 to 64 neighbouring positions
- class_head: bfloat16 [4, 3584, 256], P('tensor', 'dp'), may hold values from -0.046875 to 0.046875
Outputs:
- master_new: float32 [4096, 14336], P(('fsdp', 'dp'), 'tensor')
- first_new: bfloat16 [4096, 14336], P(('fsdp', 'dp'), 'tensor')
- second_new: bfloat16 [4096, 14336], P(('fsdp', 'dp'), 'tensor')
- teacher_new: float32 [4096, 14336], P(('fsdp', 'dp'), 'tensor')
- class_logits: float32 [2, 8, 256], P('fsdp')
Inputs may be any that keep to these rules, and one draw needn't show every extreme that they name: `pair_ids`: in every row the pair numbers never fall, and each of the 8 pairs holds 1 to 64 tokens, one of them exactly 64.
All inputs are finite; a program needn't handle non-finite values.
Results may differ from a plain program's by a relative error of at most 0.0055.
Values may be sent and summed in bfloat16 or wider, within the bound.
A program may use at most 192 MiB of HBM per device.

v0:
```python
import jax
import jax.numpy as jnp
from jax import lax
from jax.sharding import PartitionSpec as P

PAIRS = 8


beta_one = 0.9
beta_two = 0.95
learn_rate = 0.001
decay_rate = 0.1
ema_keep = 0.99


def optimizer_step(master_weight, first_moment, second_moment, teacher_weight, grad_parts):
    gradient = lax.psum_scatter(
        grad_parts[0].astype(jnp.float32).astype(jnp.bfloat16),
        "dp",
        scatter_dimension=0,
        tiled=True,
    ).astype(jnp.float32)
    first_full = beta_one * first_moment.astype(jnp.float32) + (1.0 - beta_one) * gradient
    second_full = (
        beta_two * second_moment.astype(jnp.float32) + (1.0 - beta_two) * gradient * gradient
    )
    master_new = master_weight - learn_rate * (
        first_full / (jnp.sqrt(second_full) + 1e-08) + decay_rate * master_weight
    )
    teacher_new = ema_keep * teacher_weight + (1.0 - ema_keep) * master_new
    return (
        master_new,
        first_full.astype(jnp.bfloat16),
        second_full.astype(jnp.bfloat16),
        teacher_new,
    )


def embed_inputs(embed_table, token_ids, pair_ids):
    every_id, every_pair = (
        lax.all_gather(token_ids, "fsdp", axis=0, tiled=True),
        lax.all_gather(pair_ids, "fsdp", axis=0, tiled=True),
    )
    picked = jnp.take(embed_table, every_id.reshape(-1), axis=1)
    received = lax.all_to_all(picked, "fsdp", split_axis=1, concat_axis=0, tiled=True)
    stacked = lax.all_gather(received, ("dp", "tensor"), axis=0, tiled=True)
    inner_count = lax.axis_size(("dp", "tensor"))
    shard_count = lax.axis_size("fsdp")
    piece_rows = embed_table.shape[0]
    ordered = stacked.reshape(inner_count, shard_count, piece_rows, -1).transpose(1, 0, 2, 3)
    ordered = ordered.reshape(inner_count * shard_count * piece_rows, -1)
    values = ordered.astype(jnp.float32)
    scale = lax.rsqrt(jnp.mean(values * values, axis=0, keepdims=True) + 1e-05)
    return ((values * scale).astype(jnp.bfloat16), every_pair)


def label_tokens(teacher_new, normed, every_pair, class_head):
    teacher_half = teacher_new.astype(jnp.bfloat16)
    shard_count = lax.axis_size("fsdp")
    replica_count = lax.axis_size("dp")
    place = lax.axis_index("fsdp")
    width = teacher_half.shape[1] // replica_count
    group_pairs = lax.dynamic_slice_in_dim(every_pair, place, 1, 0)
    row_block = lax.all_gather(teacher_half, "fsdp", axis=0, tiled=True)
    split_block = lax.all_to_all(row_block, "dp", split_axis=1, concat_axis=0, tiled=True)
    own_rows = teacher_half.shape[0]
    arranged = split_block.reshape(replica_count, shard_count, own_rows, -1)
    inputs = normed.reshape(shard_count, replica_count, own_rows, -1)
    hidden = jnp.einsum("fdrk,dfro->ko", inputs, arranged, preferred_element_type=jnp.float32)
    group_count = group_pairs.shape[0]
    active = jax.nn.silu(hidden).reshape(group_count, -1, width)
    member_of = (
        group_pairs[:, None, :] == jnp.arange(PAIRS, dtype=jnp.int32)[None, :, None]
    ).astype(jnp.float32)
    totals = jnp.einsum("gpt,gtk->gpk", member_of, active, precision=lax.Precision.HIGHEST)
    pooled = (totals / jnp.sum(member_of, axis=2, keepdims=True)).astype(jnp.bfloat16)
    head_part = class_head[0]
    partial_terms = jnp.einsum("gpk,kc->gpc", pooled, head_part, preferred_element_type=jnp.float32)
    partial_logits = partial_terms[0]
    return lax.psum(partial_logits, ("dp", "tensor"))[None]


def shards(
    master_weight,
    first_moment,
    second_moment,
    teacher_weight,
    grad_parts,
    embed_table,
    token_ids,
    pair_ids,
    class_head,
):
    master_new, first_new, second_new, teacher_new = optimizer_step(
        master_weight, first_moment, second_moment, teacher_weight, grad_parts
    )
    normed, every_pair = embed_inputs(embed_table, token_ids, pair_ids)
    class_logits = label_tokens(teacher_new, normed, every_pair, class_head)
    return (master_new, first_new, second_new, teacher_new, class_logits)


def solution(mesh):
    placed = (
        P(("fsdp", "dp"), "tensor"),
        P(("fsdp", "dp"), "tensor"),
        P(("fsdp", "dp"), "tensor"),
        P(("fsdp", "dp"), "tensor"),
        P("dp", "fsdp", "tensor"),
        P(("fsdp", "dp", "tensor"), None),
        P("fsdp", None),
        P("fsdp", None),
        P("tensor", "dp", None),
    )
    return jax.shard_map(
        shards,
        mesh=mesh,
        in_specs=placed,
        out_specs=(
            P(("fsdp", "dp"), "tensor"),
            P(("fsdp", "dp"), "tensor"),
            P(("fsdp", "dp"), "tensor"),
            P(("fsdp", "dp"), "tensor"),
            P("fsdp", None, None),
        ),
        check_vma=False,
    )
```

profile of v0, /device:TPU:0, one launch (start us, length us, event | category | flops | bytes accessed | tf_op | source)
XLA Modules:
  0.0 607.7 jit_solution(13864953363160223747)
XLA Ops:
  8.0 0.0 copy-start
  8.0 0.0 reduce-scatter.2.cloned.1.call-start
  8.1 0.7 reduce-scatter.2.cloned.1.call-update
  8.7 0.0 all-gather.7.cloned.1.call-start
  8.8 250.8 %reduce-scatter.2.cloned.1.call-done = bf16[512,3584]{1,0:T(8,128)(2,1)} async-done(((bf16[2048,3584]{1,0:T(8,128)(2,1)}), bf16[512,3584]{1,0:T(8,128)(2,1)}) %reduce-scatter.2.cloned.1.call-update) | async-done | bytes 3670032 | tf_op jit(solution)/shard_map/reduce_scatter | solution.py:17
  259.6 20.4 %fusion.19 = (bf16[512,3584]{1,0:T(8,128)(2,1)}, f32[512,3584]{1,0:T(8,128)}, f32[512,3584]{1,0:T(8,128)}, bf16[512,3584]{1,0:T(8,128)(2,1)}, bf16[512,3584]{1,0:T(8,128)(2,1)}) fusion(f32[512,3584]{1,0:T(8,128)} %param.12, f32[512,3584]{1,0:T(8,128)} %param.9, bf16[512,3584]{1,0:T(8,128)(2,1)} %param.11, ...), kind=kLoop, calls=%fused_computation.37 | loop fusion | flops 40370176 | bytes 51380224 | tf_op jit(solution)/shard_map/convert_element_type | solution.py:58
  280.0 0.0 all-gather.7.cloned.1.call-update
  280.1 0.0 copy-start.3
  280.1 22.3 %copy.26 = bf16[128,64128]{0,1:T(8,128)(2,1)} copy(bf16[128,64128]{1,0:T(8,128)(2,1)} %param.14) | data formatting | bytes 32833536 | tf_op args[5]
  302.3 0.0 copy-done.3
  302.3 4.2 all-gather.1
  306.6 8.8 %gather_fusion = bf16[512,128]{1,0:T(8,128)(2,1)S(1)} fusion(bf16[128,64128]{0,1:T(8,128)(2,1)} %copy.26, s32[1024]{0:T(1024)S(1)} %pad_clamp_fusion), kind=kCustom, calls=%fused_computation | custom fusion | bytes 264192 | tf_op jit(solution)/shard_map/jit(_take)/gather | solution.py:44
  315.4 0.1 copy.27
  315.6 0.7 broadcast_select_fusion
  316.2 3.4 all-to-all-start
  319.6 55.3 %all-gather.7.cloned.1.call-done = bf16[1024,3584]{1,0:T(8,128)(2,1)} async-done(((bf16[512,3584]{1,0:T(8,128)(2,1)}), bf16[1024,3584]{1,0:T(8,128)(2,1)}) %all-gather.7.cloned.1.call-update) | async-done | bytes 7340048 | tf_op jit(solution)/shard_map/all_gather | solution.py:64
  374.9 6.6 %copy.42 = bf16[128,4,8,896]{3,2,0,1:T(8,128)(2,1)} copy(bf16[128,4,8,896]{3,2,1,0:T(8,128)(2,1)} %bitcast.41) | data formatting | bytes 14680064 | tf_op jit(solution)/shard_map/all_to_all | solution.py:65
  381.5 0.0 all-to-all-done
  381.5 0.0 copy-start.2
  381.5 0.0 copy-start.4
  381.5 0.6 copy-done.2
  382.2 5.5 all-to-all-start.1
  387.7 0.0 all-gather.5.cloned.1.call-start
  387.7 0.5 all-gather.5.cloned.1.call-update
  388.2 0.0 copy-done.4
  388.3 4.2 all-gather
  392.5 0.1 convert_reduce_fusion
  392.6 73.4 %all-gather.5.cloned.1.call-done = bf16[4096,256]{1,0:T(8,128)(2,1)} async-done(((bf16[256,256]{1,0:T(8,128)(2,1)}), bf16[4096,256]{1,0:T(8,128)(2,1)}) %all-gather.5.cloned.1.call-update) | async-done | bytes 2097168 | tf_op jit(solution)/shard_map/all_gather | solution.py:46
  466.0 0.0 copy-start.1
  466.0 4.2 copy.28
  470.3 0.0 copy-done.1
  470.3 0.6 multiply_reduce_fusion
  470.8 90.4 %all-to-all-done.1 = bf16[1024,4,896]{2,0,1:T(8,128)(2,1)} async-done(((bf16[1024,4,896]{2,0,1:T(8,128)(2,1)}), bf16[1024,4,896]{2,0,1:T(8,128)(2,1)}, u32[]{:S(2)}, u32[]{:S(2)}) %all-to-all-start.1) | async-done | bytes 7340064 | tf_op jit(solution)/shard_map/all_to_all | solution.py:65
  561.2 6.7 %fusion.6 = f32[256,896]{1,0:T(8,128)S(1)} fusion(bf16[4,2,512,896]{3,2,1,0:T(8,128)(2,1)} %bitcast.14, f32[2,4,512,256]{3,2,1,0:T(8,128)} %bitcast.38, f32[256]{0:T(256)S(1)} %add_rsqrt_fusion), kind=kOutput, calls=%fused_computation.14 | convolution fusion | flops 1881145344 | bytes 12452864 | tf_op jit(solution)/shard_map/fdrk,dfro->ko/dot_general | solution.py:69
  567.9 0.6 fusion.9
  568.5 0.0 copy-done
  568.5 0.2 convolution_bitcast_fusion
  568.7 31.5 %psum.7 = f32[1,8,256]{2,1,0:T(8,128)} all-reduce(f32[1,8,256]{2,1,0:T(8,128)S(1)} %convolution_bitcast_fusion), channel_id=1, replica_groups=mesh['fsdp'=2,'dp'=4,'tensor'=4] {'dp','tensor'}, use_global_device_ids=true, to_apply=%region_3.4 | all-reduce | flops 2048 | bytes 16384 | tf_op jit(solution)/shard_map/psum | solution.py:80
  (5 shorter events, 0.0 us)
Async XLA Ops:
  8.0 560.5 %copy-start = (bf16[1,896,256]{2,1,0:T(8,128)(2,1)S(1)}, bf16[1,896,256]{2,1,0:T(8,128)(2,1)}, u32[]{:S(2)}) copy-start(bf16[1,896,256]{2,1,0:T(8,128)(2,1)} %param.17) | copy-start | bytes 1376260
  8.0 251.6 %reduce-scatter.2.cloned.1.call-start = ((), (), s32[]{:S(2)}) async-start(), calls=%async_computation.3 | async-start | bytes 18350080 | tf_op jit(solution)/shard_map/reduce_scatter | solution.py:17
  8.7 366.1 %all-gather.7.cloned.1.call-start = ((), (), s32[]{:S(2)}) async-start(), calls=%async_computation.5 | async-start | bytes 11010048 | tf_op jit(solution)/shard_map/all_gather | solution.py:64
  280.1 22.3 %copy-start.3 = (s32[1,256]{1,0:T(1,128)S(1)}, s32[1,256]{1,0:T(1,128)}, u32[]{:S(2)}) copy-start(s32[1,256]{1,0:T(1,128)} %param.15) | copy-start | bytes 3076
  316.2 65.3 %all-to-all-start = ((bf16[128,2,256]{2,0,1:T(8,128)(2,1)}), bf16[128,2,256]{2,0,1:T(8,128)(2,1)S(1)}, u32[]{:S(2)}, u32[]{:S(2)}) async-start(bf16[128,2,256]{2,0,1:T(8,128)(2,1)} %broadcast_select_fusion), calls=%async_computation.1 | async-start | bytes 262144 | tf_op jit(solution)/shard_map/all_to_all | solution.py:45
  381.5 0.7 copy-start.2
  381.5 6.7 %copy-start.4 = (s32[1,256]{1,0:T(1,128)S(1)}, s32[1,256]{1,0:T(1,128)}, u32[]{:S(2)}) copy-start(s32[1,256]{1,0:T(1,128)} %param.16) | copy-start | bytes 3076
  382.2 179.0 %all-to-all-start.1 = ((bf16[1024,4,896]{2,0,1:T(8,128)(2,1)}), bf16[1024,4,896]{2,0,1:T(8,128)(2,1)}, u32[]{:S(2)}, u32[]{:S(2)}) async-start(bf16[1024,4,896]{2,0,1:T(8,128)(2,1)} %bitcast.37), calls=%async_computation.2 | async-start | bytes 14680064 | tf_op jit(solution)/shard_map/all_to_all | solution.py:65
  387.7 78.3 %all-gather.5.cloned.1.call-start = ((), (), s32[]{:S(2)}) async-start(), calls=%async_computation.4 | async-start | bytes 2228224 | tf_op jit(solution)/shard_map/all_gather | solution.py:46
  466.0 4.2 copy-start.1
Sparse Core Ops, SparseCore 0:
  11.2 248.3 reduce-scatter.1
  280.2 94.6 all-gather.6
Sparse Core Ops, SparseCore 1:
  390.3 75.7 all-gather.4
where the time goes:
time: 609 us; the launch traced here: 608 us
  waiting for transfers between devices  471 us (77%)
  local copies, waits for them, and re-layouts  42.7 us (7%)
  blocking collectives  40 us (7%)
  other arithmetic  21.8 us (4%)
  between operations  15.6 us (3%)
  starting transfers between devices  8.99 us (1%)
  matrix products  7.5 us (1%)
    reduce_scatter x1, waiting for transfers between devices, optimizer_step(): lax.psum_scatter(grad_parts[0].astype(jnp.float32).astype(jnp.bfloat16),...  251 us
    all_to_all x1, waiting for transfers between devices, label_tokens(): lax.all_to_all(row_block, 'dp', split_axis=1, concat_axis=0, tiled=True)  90.4 us
    all_gather x1, waiting for transfers between devices, embed_inputs(): stacked = lax.all_gather(received, ('dp', 'tensor'), axis=0, tiled=True)  73.4 us
    all_gather x1, waiting for transfers between devices, label_tokens(): row_block = lax.all_gather(teacher_half, 'fsdp', axis=0, tiled=True)  55.3 us
    psum x1, blocking collectives, label_tokens(): return lax.psum(partial_logits, ('dp', 'tensor'))[None]  31.5 us
    unnamed x11, local copies, waits for them, and re-layouts  22.9 us
    convert_element_type x1, other arithmetic, label_tokens(): teacher_half = teacher_new.astype(jnp.bfloat16)  20.4 us
  transfers between devices with their start and end apart: 5, of which 4 were waited for; matrix products, arithmetic and copies ran while one was open for 7% of the time, Pallas kernels for 0%

commit v1 on v0

v1 whole, which is shorter than its diff:
```python
import jax
import jax.numpy as jnp
from jax import lax
from jax.sharding import PartitionSpec as P

PAIRS = 8


beta_one = 0.9
beta_two = 0.95
learn_rate = 0.001
decay_rate = 0.1
ema_keep = 0.99


def spread(block, axes):
    count = lax.axis_size(axes)
    copies = jnp.broadcast_to(block[None], (count,) + block.shape)
    return lax.all_to_all(copies, axes, split_axis=0, concat_axis=0, tiled=True)


def update(master_weight, first_moment, second_moment, teacher_weight, gradient):
    gradient = gradient.astype(jnp.float32)
    first_full = beta_one * first_moment.astype(jnp.float32) + (1.0 - beta_one) * gradient
    second_full = (
        beta_two * second_moment.astype(jnp.float32) + (1.0 - beta_two) * gradient * gradient
    )
    master_new = master_weight - learn_rate * (
        first_full / (jnp.sqrt(second_full) + 1e-08) + decay_rate * master_weight
    )
    teacher_new = ema_keep * teacher_weight + (1.0 - ema_keep) * master_new
    return (
        master_new,
        first_full.astype(jnp.bfloat16),
        second_full.astype(jnp.bfloat16),
        teacher_new,
    )


def own_features(embed_table, token_ids):
    every_id = spread(token_ids, "fsdp").reshape(-1)
    picked = jnp.take(embed_table, every_id, axis=1)
    rows = spread(picked, "tensor").reshape(-1, every_id.shape[0])
    values = rows.astype(jnp.float32)
    squares = spread(jnp.sum(values * values, axis=0), ("fsdp", "dp"))
    features = rows.shape[0] * squares.shape[0]
    scale = lax.rsqrt(jnp.sum(squares, axis=0, keepdims=True) / features + 1e-05)
    return (values * scale).astype(jnp.bfloat16)


def shards(
    master_weight,
    first_moment,
    second_moment,
    teacher_weight,
    grad_parts,
    embed_table,
    token_ids,
    pair_ids,
    class_head,
):
    replicas = lax.axis_size("dp")
    groups = lax.axis_size("fsdp")
    tokens = token_ids.shape[1]
    width = master_weight.shape[1] // replicas
    head_part = class_head[0]
    partial = grad_parts[0]

    steps = [256] * (width // 256) + ([width % 256] if width % 256 else [])
    bounds = [(sum(steps[:i]), sum(steps[: i + 1])) for i in range(len(steps))]

    def columns(whole, low, high):
        return [whole[:, d * width + low : d * width + high] for d in range(replicas)]

    pieces = [
        lax.psum_scatter(
            jnp.concatenate(columns(partial, low, high), axis=1),
            "dp",
            scatter_dimension=0,
            tiled=True,
        )
        for low, high in bounds
    ]

    normed = own_features(embed_table, token_ids)
    member_of = (
        pair_ids[0][None, :] == jnp.arange(PAIRS, dtype=jnp.int32)[:, None]
    ).astype(jnp.float32)
    sizes = jnp.sum(member_of, axis=1, keepdims=True)

    terms = jnp.zeros((PAIRS, head_part.shape[1]), jnp.float32)
    for (low, high), piece in zip(bounds, pieces):
        step = high - low
        halves = [
            update(*own)[3].astype(jnp.bfloat16)
            for own in zip(
                columns(master_weight, low, high),
                columns(first_moment, low, high),
                columns(second_moment, low, high),
                columns(teacher_weight, low, high),
                [piece[:, d * step : (d + 1) * step] for d in range(replicas)],
            )
        ]
        teacher_half = jnp.stack(halves)
        sent = jnp.einsum(
            "fk,dfw->dkw", normed, teacher_half, preferred_element_type=jnp.float32
        ).astype(jnp.bfloat16)
        sent = sent.reshape(replicas * groups, tokens, step)
        received = lax.all_to_all(
            sent, ("dp", "fsdp"), split_axis=0, concat_axis=0, tiled=True
        )
        hidden = jnp.sum(received.astype(jnp.float32), axis=0)
        active = jax.nn.silu(hidden)
        totals = jnp.dot(member_of, active, precision=lax.Precision.HIGHEST)
        pooled = (totals / sizes).astype(jnp.bfloat16)
        terms = terms + jnp.dot(
            pooled, head_part[low:high], preferred_element_type=jnp.float32
        )

    gradient = jnp.concatenate(
        [
            piece[:, d * (high - low) : (d + 1) * (high - low)]
            for d in range(replicas)
            for (low, high), piece in zip(bounds, pieces)
        ],
        axis=1,
    )
    updated = update(master_weight, first_moment, second_moment, teacher_weight, gradient)
    logits = jnp.sum(spread(terms, ("dp", "tensor")), axis=0)[None]
    return (*updated, logits)


def solution(mesh):
    placed = (
        P(("fsdp", "dp"), "tensor"),
        P(("fsdp", "dp"), "tensor"),
        P(("fsdp", "dp"), "tensor"),
        P(("fsdp", "dp"), "tensor"),
        P("dp", "fsdp", "tensor"),
        P(("fsdp", "dp", "tensor"), None),
        P("fsdp", None),
        P("fsdp", None),
        P("tensor", "dp", None),
    )
    return jax.shard_map(
        shards,
        mesh=mesh,
        in_specs=placed,
        out_specs=(
            P(("fsdp", "dp"), "tensor"),
            P(("fsdp", "dp"), "tensor"),
            P(("fsdp", "dp"), "tensor"),
            P(("fsdp", "dp"), "tensor"),
            P("fsdp", None, None),
        ),
        check_vma=False,
    )
```

time: 609 us -> 486 us (0.80)
  waiting for transfers between devices: 471 us -> 219 us
  local copies, waits for them, and re-layouts: 42.7 us -> 142 us
  other arithmetic: 21.8 us -> 54.9 us
  blocking collectives: 40 us -> 11.9 us
  starting transfers between devices: 8.99 us -> 33.5 us
    all_gather x2 -> x0, waiting for transfers between devices: 129 us -> none  [the longest x1 73.4 us: embed_inputs(): stacked = lax.all_gather(received, ('dp', 'tensor'), axis=0, tiled=True)]
    reduce_scatter x1 -> x4, waiting for transfers between devices: 251 us -> 152 us  [shards(): lax.psum_scatter(jnp.concatenate(columns(partial, low, high), axis=1), 'd...]
    unnamed x11 -> x51, local copies, waits for them, and re-layouts: 22.9 us -> 114 us
    psum x1 -> x0, blocking collectives: 31.5 us -> none  [label_tokens(): return lax.psum(partial_logits, ('dp', 'tensor'))[None]]
    all_to_all x2 -> x7, starting transfers between devices: 8.87 us -> 33.4 us  [the longest x4 19.6 us: shards(): lax.all_to_all(sent, ('dp', 'fsdp'), split_axis=0, concat_axis=0, tiled=T...]
    all_to_all x2 -> x7, waiting for transfers between devices: 90.4 us -> 66.9 us  [the longest x4 66.9 us: shards(): lax.all_to_all(sent, ('dp', 'fsdp'), split_axis=0, concat_axis=0, tiled=T...]
    another operation x0 -> x6, other arithmetic: none -> 21 us  [shards(): teacher_half = jnp.stack(halves)]
    convert_element_type x1, other arithmetic: 20.4 us -> 0.09 us  [own_features(): return (values * scale).astype(jnp.bfloat16)]
  transfers between devices with their start and end apart: 5 -> 11, of which waited for: 4 -> 6; matrix products, arithmetic and copies ran while one was open for 7% -> 35% of each run, Pallas kernels for 0% -> 0%
where the time goes in v1:
time: 486 us; the launch traced here: 483 us
  waiting for transfers between devices  219 us (45%)
  local copies, waits for them, and re-layouts  142 us (29%)
  other arithmetic  54.9 us (11%)
  starting transfers between devices  33.5 us (7%)
  between operations  14 us (3%)
  blocking collectives  11.9 us (2%)
  matrix products  7.22 us (1%)
    reduce_scatter x4, waiting for transfers between devices, shards(): lax.psum_scatter(jnp.concatenate(columns(partial, low, high), axis=1), 'd...  152 us
    unnamed x51, local copies, waits for them, and re-layouts  114 us
    all_to_all x4, waiting for transfers between devices, shards(): lax.all_to_all(sent, ('dp', 'fsdp'), split_axis=0, concat_axis=0, tiled=T...  66.9 us
    another operation x6, other arithmetic, shards(): teacher_half = jnp.stack(halves)  21 us
    all_to_all x4, starting transfers between devices, shards(): lax.all_to_all(sent, ('dp', 'fsdp'), split_axis=0, concat_axis=0, tiled=T...  19.6 us
    add x1, other arithmetic, update(): teacher_new = ema_keep * teacher_weight + (1.0 - ema_keep) * master_new  17.6 us
    all_to_all x3, starting transfers between devices, spread(): return lax.all_to_all(copies, axes, split_axis=0, concat_axis=0, tiled=True)  13.8 us
    all_to_all x1, blocking collectives, spread(): return lax.all_to_all(copies, axes, split_axis=0, concat_axis=0, tiled=True)  11.9 us
  transfers between devices with their start and end apart: 11, of which 6 were waited for; matrix products, arithmetic and copies ran while one was open for 35% of the time, Pallas kernels for 0%

profile of v1, /device:TPU:0, one launch (start us, length us, event | category | flops | bytes accessed | tf_op | source)
XLA Modules:
  0.0 483.1 jit_solution(17786495291362714369)
XLA Ops:
  7.2 20.4 %copy.251 = bf16[1,2048,3584]{1,2,0:T(8,128)(2,1)} copy(bf16[1,2048,3584]{2,1,0:T(8,128)(2,1)} %param.13) | data formatting | bytes 29360128 | tf_op args[4]
  27.6 1.8 fusion.282
  29.3 1.6 pad_maximum_fusion.3
  31.0 7.5 %fusion.283 = (bf16[2048,256]{0,1:T(8,128)(2,1)}, bf16[2048,256]{0,1:T(8,128)(2,1)}, bf16[2048,256]{0,1:T(8,128)(2,1)}, bf16[2048,256]{0,1:T(8,128)(2,1)}, bf16[...) fusion(bf16[2048,3584]{0,1:T(8,128)(2,1)} %bitcast.83), kind=kLoop, calls=%fused_computation.381 | loop fusion | bytes 25165824 | tf_op jit(solution)/shard_map/slice | solution.py:73
  38.5 2.3 pad_maximum_fusion
  40.9 3.7 pad_maximum_fusion.2
  44.6 3.3 pad_maximum_fusion.1
  49.2 4.2 all-to-all-start
  53.4 22.1 %copy.272 = bf16[128,64128]{0,1:T(8,128)(2,1)} copy(bf16[128,64128]{1,0:T(8,128)(2,1)} %param.14) | data formatting | bytes 32833536 | tf_op args[5]
  75.5 8.9 %gather_fusion = bf16[512,128]{1,0:T(8,128)(2,1)S(1)} fusion(bf16[128,64128]{0,1:T(8,128)(2,1)} %copy.272, s32[1024]{0:T(1024)S(1)} %pad_clamp_fusion), kind=kCustom, calls=%fused_computation | custom fusion | bytes 264192 | tf_op jit(solution)/shard_map/jit(_take)/gather | solution.py:42
  84.7 11.9 %all_to_all.41 = bf16[4,128,512]{2,1,0:T(8,128)(2,1)S(1)} all-to-all(bf16[4,128,512]{2,1,0:T(8,128)(2,1)S(1)} %broadcast_in_dim.46), channel_id=1, replica_groups=mesh['fsdp'=2,'dp'=4,'tensor'=4] {'tensor'}, dimensions={0} | all-to-all | bytes 1048576 | tf_op jit(solution)/shard_map/all_to_all | solution.py:19
  97.3 5.9 %all-to-all-start.2 = ((f32[8,1,512]{2,1,0:T(1,128)}), f32[8,1,512]{2,1,0:T(1,128)S(1)}, u32[]{:S(2)}, u32[]{:S(2)}) async-start(f32[8,1,512]{2,1,0:T(1,128)} %broadcast_in_dim.47), calls=%async_computation.6 | async-start | bytes 32768 | tf_op jit(solution)/shard_map/all_to_all | solution.py:19
  103.2 6.0 %copy.250 = bf16[512,3584]{0,1:T(8,128)(2,1)} copy(bf16[512,3584]{1,0:T(8,128)(2,1)} %param.10) | data formatting | bytes 7340032 | tf_op args[1]
  109.2 5.9 %copy.252 = bf16[512,3584]{0,1:T(8,128)(2,1)} copy(bf16[512,3584]{1,0:T(8,128)(2,1)} %param.11) | data formatting | bytes 7340032 | tf_op args[2]
  115.1 8.4 %copy.254 = f32[512,3584]{0,1:T(8,128)} copy(f32[512,3584]{1,0:T(8,128)} %param.9) | data formatting | bytes 14680064 | tf_op args[0]
  123.5 8.4 %copy.255 = f32[512,3584]{0,1:T(8,128)} copy(f32[512,3584]{1,0:T(8,128)} %param.12) | data formatting | bytes 14680064 | tf_op args[3]
  132.0 1.6 fusion.264
  133.6 2.5 fusion.263
  136.6 1.0 copy.326
  137.6 6.0 %all-to-all-start.6 = ((bf16[8,256,128]{2,1,0:T(8,128)(2,1)}), bf16[8,256,128]{2,1,0:T(8,128)(2,1)S(1)}, u32[]{:S(2)}, u32[]{:S(2)}) async-start(bf16[8,256,128]{2,1,0:T(8,128)(2,1)} %bitcast.35), calls=%async_computation.10 | async-start | bytes 1048576 | tf_op jit(solution)/shard_map/all_to_all | solution.py:109
  143.6 23.6 %all-to-all-done.6 = bf16[8,256,128]{2,1,0:T(8,128)(2,1)S(1)} async-done(((bf16[8,256,128]{2,1,0:T(8,128)(2,1)}), bf16[8,256,128]{2,1,0:T(8,128)(2,1)S(1)}, u32[]{:S(2)}, u32[]{:S(2)}) %all-to-all-start.6) | async-done | bytes 524320 | tf_op jit(solution)/shard_map/all_to_all | solution.py:109
  167.6 4.8 fusion.236
  172.4 72.8 %reduce-scatter.9.cloned.1.call-done = bf16[512,1024]{0,1:T(8,128)(2,1)} async-done(((bf16[2048,1024]{0,1:T(8,128)(2,1)}), bf16[512,1024]{0,1:T(8,128)(2,1)}) %reduce-scatter.9.cloned.1.call-update) | async-done | bytes 1048592 | tf_op jit(solution)/shard_map/reduce_scatter | solution.py:76
  245.2 79.5 %reduce-scatter.7.cloned.1.call-done = bf16[512,1024]{0,1:T(8,128)(2,1)} async-done(((bf16[2048,1024]{0,1:T(8,128)(2,1)}), bf16[512,1024]{0,1:T(8,128)(2,1)}) %reduce-scatter.7.cloned.1.call-update) | async-done | bytes 1048592 | tf_op jit(solution)/shard_map/reduce_scatter | solution.py:76
  324.7 4.6 fusion.245
  329.4 1.8 fusion.4
  331.2 1.3 copy.275
  332.5 5.1 %all-to-all-start.3 = ((bf16[8,256,256]{2,1,0:T(8,128)(2,1)}), bf16[8,256,256]{2,1,0:T(8,128)(2,1)}, u32[]{:S(2)}, u32[]{:S(2)}) async-start(bf16[8,256,256]{2,1,0:T(8,128)(2,1)} %bitcast.14), calls=%async_computation.7 | async-start | bytes 2097152 | tf_op jit(solution)/shard_map/all_to_all | solution.py:109
  337.7 3.8 fusion.240
  341.5 1.7 fusion.5
  343.2 2.2 copy.292
  345.4 3.8 fusion.244
  349.2 1.7 fusion.6
  350.9 2.3 copy.309
  353.1 0.7 slice_dynamic-update-slice_fusion.11
  353.9 0.7 slice_dynamic-update-slice_fusion.10
  354.6 0.7 slice_dynamic-update-slice_fusion.9
  355.3 8.3 %all-to-all-done.3 = bf16[8,256,256]{2,1,0:T(8,128)(2,1)} async-done(((bf16[8,256,256]{2,1,0:T(8,128)(2,1)}), bf16[8,256,256]{2,1,0:T(8,128)(2,1)}, u32[]{:S(2)}, u32[]{:S(2)}) %all-to-all-start.3) | async-done | bytes 1048608 | tf_op jit(solution)/shard_map/all_to_all | solution.py:109
  363.6 4.2 all-to-all-start.5
  367.8 1.6 slice_dynamic-update-slice_fusion.15
  369.4 0.7 slice_dynamic-update-slice_fusion.8
  370.1 0.7 slice_dynamic-update-slice_fusion.7
  370.8 0.7 slice_dynamic-update-slice_fusion.6
  371.6 1.6 slice_dynamic-update-slice_fusion.14
  373.1 0.7 slice_dynamic-update-slice_fusion.5
  373.8 0.7 slice_dynamic-update-slice_fusion.4
  374.6 0.7 slice_dynamic-update-slice_fusion.3
  375.3 18.2 %all-to-all-done.5 = bf16[8,256,256]{2,1,0:T(8,128)(2,1)} async-done(((bf16[8,256,256]{2,1,0:T(8,128)(2,1)}), bf16[8,256,256]{2,1,0:T(8,128)(2,1)}, u32[]{:S(2)}, u32[]{:S(2)}) %all-to-all-start.5) | async-done | bytes 1048608 | tf_op jit(solution)/shard_map/all_to_all | solution.py:109
  393.5 4.2 all-to-all-start.4
  397.7 1.6 slice_dynamic-update-slice_fusion.13
  399.3 0.7 slice_dynamic-update-slice_fusion.2
  400.0 0.7 slice_dynamic-update-slice_fusion.1
  400.7 0.7 slice_dynamic-update-slice_fusion
  401.4 1.6 slice_dynamic-update-slice_fusion.12
  403.0 1.4 convert_reduce_fusion.2
  404.4 1.4 convert_reduce_fusion
  406.3 16.9 %all-to-all-done.4 = bf16[8,256,256]{2,1,0:T(8,128)(2,1)} async-done(((bf16[8,256,256]{2,1,0:T(8,128)(2,1)}), bf16[8,256,256]{2,1,0:T(8,128)(2,1)}, u32[]{:S(2)}, u32[]{:S(2)}) %all-to-all-start.4) | async-done | bytes 1048608 | tf_op jit(solution)/shard_map/all_to_all | solution.py:109
  423.1 1.4 convert_reduce_fusion.1
  426.0 3.7 all-to-all-start.7
  429.8 17.6 %multiply_add_fusion = (f32[512,3584]{0,1:T(8,128)}, f32[512,3584]{0,1:T(8,128)}, bf16[512,3584]{0,1:T(8,128)(2,1)}, bf16[512,3584]{0,1:T(8,128)(2,1)}) fusion(f32[512,3584]{0,1:T(8,128)} %copy.255, f32[512,3584]{0,1:T(8,128)} %copy.254, bf16[512,3584]{0,1:T(8,128)(2,1)} %copy.252, bf16[512,3584]{0,1:T(8,128)(2,1)} %slice_dynamic-update-slice_fusion.12, ...), kind=kLoop, calls=%fused_computation.5 | loop fusion | flops 38535168 | bytes 47710208 | tf_op jit(solution)/shard_map/add | solution.py:31
  447.4 8.4 %copy.330 = f32[512,3584]{1,0:T(8,128)} copy(f32[512,3584]{0,1:T(8,128)} %get-tuple-element.25) | data formatting | bytes 14680064
  455.7 5.9 %copy.329 = bf16[512,3584]{1,0:T(8,128)(2,1)} copy(bf16[512,3584]{0,1:T(8,128)(2,1)} %get-tuple-element.58) | data formatting | bytes 7340032
  461.6 5.9 %copy.328 = bf16[512,3584]{1,0:T(8,128)(2,1)} copy(bf16[512,3584]{0,1:T(8,128)(2,1)} %get-tuple-element.59) | data formatting | bytes 7340032
  467.6 8.4 %copy.327 = f32[512,3584]{1,0:T(8,128)} copy(f32[512,3584]{0,1:T(8,128)} %get-tuple-element.26) | data formatting | bytes 14680064
  (64 shorter events, 6.2 us)
Async XLA Ops:
  7.2 124.8 %reduce-scatter.11.cloned.1.call-start = ((), (), s32[]{:S(2)}) async-start(), calls=%async_computation.15 | async-start | bytes 2621440 | tf_op jit(solution)/shard_map/reduce_scatter | solution.py:76
  30.9 136.6 %reduce-scatter.5.cloned.1.call-start = ((), (), s32[]{:S(2)}) async-start(), calls=%async_computation.12 | async-start | bytes 5242880 | tf_op jit(solution)/shard_map/reduce_scatter | solution.py:76
  40.8 204.3 %reduce-scatter.9.cloned.1.call-start = ((), (), s32[]{:S(2)}) async-start(), calls=%async_computation.14 | async-start | bytes 5242880 | tf_op jit(solution)/shard_map/reduce_scatter | solution.py:76
  44.6 280.1 %reduce-scatter.7.cloned.1.call-start = ((), (), s32[]{:S(2)}) async-start(), calls=%async_computation.13 | async-start | bytes 5242880 | tf_op jit(solution)/shard_map/reduce_scatter | solution.py:76
  47.9 0.7 copy-start.11
  49.2 26.3 %all-to-all-start = ((s32[2,1,256]{2,1,0:T(1,128)}), s32[2,1,256]{2,1,0:T(1,128)S(1)}, u32[]{:S(2)}, u32[]{:S(2)}) async-start(s32[2,1,256]{2,1,0:T(1,128)} %broadcast_in_dim.23), calls=%async_computation.4 | async-start | bytes 4096 | tf_op jit(solution)/shard_map/all_to_all | solution.py:19
  97.3 34.5 %all-to-all-start.2 = ((f32[8,1,512]{2,1,0:T(1,128)}), f32[8,1,512]{2,1,0:T(1,128)S(1)}, u32[]{:S(2)}, u32[]{:S(2)}) async-start(f32[8,1,512]{2,1,0:T(1,128)} %broadcast_in_dim.47), calls=%async_computation.6 | async-start | bytes 32768 | tf_op jit(solution)/shard_map/all_to_all | solution.py:19
  132.0 5.6 %copy-start.3 = (bf16[512,512]{1,0:T(8,128)(2,1)}, bf16[512,512]{1,0:T(8,128)(2,1)S(1)}, u32[]{:S(2)}) copy-start(bf16[512,512]{1,0:T(8,128)(2,1)S(1)} %fusion.33) | copy-start | bytes 1572868
  133.6 9.9 %copy-start.12 = (s32[1,256]{1,0:T(1,128)S(1)}, s32[1,256]{1,0:T(1,128)}, u32[]{:S(2)}) copy-start(s32[1,256]{1,0:T(1,128)} %param.16) | copy-start | bytes 3076
  137.6 29.7 %all-to-all-start.6 = ((bf16[8,256,128]{2,1,0:T(8,128)(2,1)}), bf16[8,256,128]{2,1,0:T(8,128)(2,1)S(1)}, u32[]{:S(2)}, u32[]{:S(2)}) async-start(bf16[8,256,128]{2,1,0:T(8,128)(2,1)} %bitcast.35), calls=%async_computation.10 | async-start | bytes 1048576 | tf_op jit(solution)/shard_map/all_to_all | solution.py:109
  167.6 157.1 %copy-start = (bf16[512,1024]{0,1:T(8,128)(2,1)S(1)}, bf16[512,1024]{0,1:T(8,128)(2,1)}, u32[]{:S(2)}) copy-start(bf16[512,1024]{0,1:T(8,128)(2,1)} %reduce-scatter.5.cloned.1.call-done) | copy-start | bytes 3145732
  324.7 4.6 copy-start.8
  324.7 4.6 copy-start.9
  324.7 4.6 copy-start.10
  329.3 8.3 %copy-start.2 = (bf16[512,1024]{0,1:T(8,128)(2,1)S(1)}, bf16[512,1024]{0,1:T(8,128)(2,1)}, u32[]{:S(2)}) copy-start(bf16[512,1024]{0,1:T(8,128)(2,1)} %reduce-scatter.7.cloned.1.call-done) | copy-start | bytes 3145732
  332.5 31.1 %all-to-all-start.3 = ((bf16[8,256,256]{2,1,0:T(8,128)(2,1)}), bf16[8,256,256]{2,1,0:T(8,128)(2,1)}, u32[]{:S(2)}, u32[]{:S(2)}) async-start(bf16[8,256,256]{2,1,0:T(8,128)(2,1)} %bitcast.14), calls=%async_computation.7 | async-start | bytes 2097152 | tf_op jit(solution)/shard_map/all_to_all | solution.py:109
  337.6 3.8 copy-start.4
  337.7 3.8 copy-start.7
  341.4 4.0 copy-start.1
  345.4 3.8 copy-start.5
  363.6 29.9 %all-to-all-start.5 = ((bf16[8,256,256]{2,1,0:T(8,128)(2,1)}), bf16[8,256,256]{2,1,0:T(8,128)(2,1)}, u32[]{:S(2)}, u32[]{:S(2)}) async-start(bf16[8,256,256]{2,1,0:T(8,128)(2,1)} %bitcast.85), calls=%async_computation.9 | async-start | bytes 2097152 | tf_op jit(solution)/shard_map/all_to_all | solution.py:109
  393.5 29.7 %all-to-all-start.4 = ((bf16[8,256,256]{2,1,0:T(8,128)(2,1)}), bf16[8,256,256]{2,1,0:T(8,128)(2,1)}, u32[]{:S(2)}, u32[]{:S(2)}) async-start(bf16[8,256,256]{2,1,0:T(8,128)(2,1)} %bitcast.84), calls=%async_computation.8 | async-start | bytes 2097152 | tf_op jit(solution)/shard_map/all_to_all | solution.py:109
  400.7 24.0 %copy-start.6 = (bf16[1,896,256]{2,1,0:T(8,128)(2,1)S(1)}, bf16[1,896,256]{2,1,0:T(8,128)(2,1)}, u32[]{:S(2)}) copy-start(bf16[1,896,256]{2,1,0:T(8,128)(2,1)} %param.17) | copy-start | bytes 1376260
  426.0 49.9 %all-to-all-start.7 = ((f32[16,8,256]{2,1,0:T(8,128)}), f32[16,8,256]{2,1,0:T(8,128)S(1)}, u32[]{:S(2)}, u32[]{:S(2)}) async-start(f32[16,8,256]{2,1,0:T(8,128)} %broadcast_in_dim.48), calls=%async_computation.11 | async-start | bytes 262144 | tf_op jit(solution)/shard_map/all_to_all | solution.py:19
Sparse Core Ops, SparseCore 0:
  31.0 46.5 reduce-scatter.10
  80.0 83.1 reduce-scatter.4
  165.5 79.6 reduce-scatter.8
  247.4 77.2 reduce-scatter.6

commit v2 on v1

--- a/solution.py
+++ b/solution.py
@@ -1,6 +1,7 @@
 import jax
 import jax.numpy as jnp
 from jax import lax
+from jax.experimental.layout import Layout, with_layout_constraint
 from jax.sharding import PartitionSpec as P
 
 PAIRS = 8
@@ -11,6 +12,10 @@
 learn_rate = 0.001
 decay_rate = 0.1
 ema_keep = 0.99
+
+
+def row_major(block):
+    return with_layout_constraint(block, Layout(major_to_minor=tuple(range(block.ndim))))
 
 
 def spread(block, axes):
@@ -73,26 +78,32 @@
         return [whole[:, d * width + low : d * width + high] for d in range(replicas)]
 
     pieces = [
-        lax.psum_scatter(
-            jnp.concatenate(columns(partial, low, high), axis=1),
-            "dp",
-            scatter_dimension=0,
-            tiled=True,
+        row_major(
+            lax.psum_scatter(
+                row_major(jnp.concatenate(columns(partial, low, high), axis=1)),
+                "dp",
+                scatter_dimension=0,
+                tiled=True,
+            )
         )
         for low, high in bounds
     ]
 
     normed = own_features(embed_table, token_ids)
+    turned = row_major(normed.T)
     member_of = (
         pair_ids[0][None, :] == jnp.arange(PAIRS, dtype=jnp.int32)[:, None]
     ).astype(jnp.float32)
     sizes = jnp.sum(member_of, axis=1, keepdims=True)
 
     terms = jnp.zeros((PAIRS, head_part.shape[1]), jnp.float32)
-    for (low, high), piece in zip(bounds, pieces):
+    for at, (low, high) in enumerate(bounds):
         step = high - low
+        if at:
+            terms, pieces[at] = lax.optimization_barrier((terms, pieces[at]))
+        piece = pieces[at]
         halves = [
-            update(*own)[3].astype(jnp.bfloat16)
+            row_major(update(*own)[3].astype(jnp.bfloat16))
             for own in zip(
                 columns(master_weight, low, high),
                 columns(first_moment, low, high),
@@ -101,11 +112,19 @@
                 [piece[:, d * step : (d + 1) * step] for d in range(replicas)],
             )
         ]
-        teacher_half = jnp.stack(halves)
-        sent = jnp.einsum(
-            "fk,dfw->dkw", normed, teacher_half, preferred_element_type=jnp.float32
-        ).astype(jnp.bfloat16)
-        sent = sent.reshape(replicas * groups, tokens, step)
+        sent = jnp.concatenate(
+            [
+                lax.dot_general(
+                    turned,
+                    half,
+                    (((1,), (0,)), ((), ())),
+                    preferred_element_type=jnp.float32,
+                ).astype(jnp.bfloat16)
+                for half in halves
+            ],
+            axis=0,
+        )
+        sent = row_major(sent.reshape(replicas * groups, tokens, step))
         received = lax.all_to_all(
             sent, ("dp", "fsdp"), split_axis=0, concat_axis=0, tiled=True
         )

time: 486 us -> 436 us (0.90)
  local copies, waits for them, and re-layouts: 142 us -> 63.1 us
  matrix products: 7.22 us -> 34 us
  other arithmetic: 54.9 us -> 34.1 us
  blocking collectives: 11.9 us -> 25 us
  waiting for transfers between devices: 219 us -> 227 us
    all_to_all x4, waiting for transfers between devices: 66.9 us -> 162 us  [shards(): lax.all_to_all(sent, ('dp', 'fsdp'), split_axis=0, concat_axis=0, tiled=T...]
    reduce_scatter x4, waiting for transfers between devices: 152 us -> 64.5 us  [shards(): lax.psum_scatter(row_major(jnp.concatenate(columns(partial, low, high), a...]
    unnamed x51 -> x30, local copies, waits for them, and re-layouts: 114 us -> 43.1 us
    dot_general x4 -> x16, matrix products: 5.67 us -> 32.5 us  [shards(): lax.dot_general(turned, half, (((1,), (0,)), ((), ())), preferred_element...]
    another operation x6 -> x0, other arithmetic: 21 us -> none  [shards(): teacher_half = jnp.stack(halves)]
    all_to_all x1 -> x2, blocking collectives: 11.9 us -> 25 us  [spread(): return lax.all_to_all(copies, axes, split_axis=0, concat_axis=0, tiled=True)]
    all_to_all x4, starting transfers between devices: 19.6 us -> 29.2 us  [shards(): lax.all_to_all(sent, ('dp', 'fsdp'), split_axis=0, concat_axis=0, tiled=T...]
    convert_element_type x4 -> x0, local copies, waits for them, and re-layouts: 6.82 us -> none  [shards(): sent = jnp.einsum('fk,dfw->dkw', normed, teacher_half, preferred_element_...]
  transfers between devices with their start and end apart: 11 -> 10, of which waited for: 6 -> 7; matrix products, arithmetic and copies ran while one was open for 35% -> 23% of each run, Pallas kernels for 0% -> 0%
where the time goes in v2:
time: 436 us; the launch traced here: 434 us
  waiting for transfers between devices  227 us (52%)
  local copies, waits for them, and re-layouts  63.1 us (14%)
  starting transfers between devices  37.1 us (9%)
  other arithmetic  34.1 us (8%)
  matrix products  34 us (8%)
  blocking collectives  25 us (6%)
  between operations  14 us (3%)
    all_to_all x4, waiting for transfers between devices, shards(): lax.all_to_all(sent, ('dp', 'fsdp'), split_axis=0, concat_axis=0, tiled=T...  162 us
    reduce_scatter x4, waiting for transfers between devices, shards(): lax.psum_scatter(row_major(jnp.concatenate(columns(partial, low, high), a...  64.5 us
    unnamed x30, local copies, waits for them, and re-layouts  43.1 us
    dot_general x16, matrix products, shards(): lax.dot_general(turned, half, (((1,), (0,)), ((), ())), preferred_element...  32.5 us
    all_to_all x4, starting transfers between devices, shards(): lax.all_to_all(sent, ('dp', 'fsdp'), split_axis=0, concat_axis=0, tiled=T...  29.2 us
    all_to_all x2, blocking collectives, spread(): return lax.all_to_all(copies, axes, split_axis=0, concat_axis=0, tiled=True)  25 us
    add x1, other arithmetic, update(): teacher_new = ema_keep * teacher_weight + (1.0 - ema_keep) * master_new  17.6 us
    concatenate x4, other arithmetic, shards(): jnp.concatenate(columns(partial, low, high), axis=1)  11 us
  transfers between devices with their start and end apart: 10, of which 7 were waited for; matrix products, arithmetic and copies ran while one was open for 23% of the time, Pallas kernels for 0%

profile of v2, /device:TPU:0, one launch (start us, length us, event | category | flops | bytes accessed | tf_op | source)
XLA Modules:
  0.0 434.3 jit_solution(1710742029906059240)
XLA Ops:
  7.2 7.4 %fusion.389 = (bf16[2048,256]{1,0:T(8,128)(2,1)S(1)}, bf16[2048,256]{1,0:T(8,128)(2,1)S(1)}, bf16[2048,256]{1,0:T(8,128)(2,1)S(1)}, bf16[2048,256]{1,0:T(8,128)(...) fusion(bf16[2048,3584]{1,0:T(8,128)(2,1)} %bitcast.200), kind=kLoop, calls=%fused_computation.472 | loop fusion | bytes 25165824 | tf_op jit(solution)/shard_map/slice | solution.py:78
  14.6 2.3 pad_maximum_fusion
  17.0 3.8 pad_maximum_fusion.1
  20.9 0.7 copy-done.5
  21.5 0.6 broadcast_in_dim.23
  22.1 4.2 all-to-all-start
  26.3 3.3 pad_maximum_fusion.2
  29.7 22.2 %copy.19 = bf16[128,64128]{0,1:T(8,128)(2,1)} copy(bf16[128,64128]{1,0:T(8,128)(2,1)} %param.14) | data formatting | bytes 32833536 | tf_op args[5]
  51.9 8.9 %gather_fusion = bf16[512,128]{1,0:T(8,128)(2,1)S(1)} fusion(bf16[128,64128]{0,1:T(8,128)(2,1)} %copy.19, s32[1024]{0:T(1024)S(1)} %pad_clamp_fusion), kind=kCustom, calls=%fused_computation | custom fusion | bytes 264192 | tf_op jit(solution)/shard_map/jit(_take)/gather | solution.py:47
  61.1 11.9 %all_to_all.41 = bf16[4,128,512]{1,2,0:T(8,128)(2,1)S(1)} all-to-all(bf16[4,128,512]{1,2,0:T(8,128)(2,1)S(1)} %broadcast_in_dim.46), channel_id=1, replica_groups=mesh['fsdp'=2,'dp'=4,'tensor'=4] {'tensor'}, dimensions={0} | all-to-all | bytes 1048576 | tf_op jit(solution)/shard_map/all_to_all | solution.py:24
  73.2 13.1 %all_to_all.42 = f32[8,1,512]{2,1,0:T(1,128)S(1)} all-to-all(f32[8,1,512]{2,1,0:T(1,128)S(1)} %broadcast_in_dim.47), channel_id=1, replica_groups=mesh['fsdp'=2,'dp'=4,'tensor'=4] {'fsdp','dp'}, dimensions={0} | all-to-all | bytes 32768 | tf_op jit(solution)/shard_map/all_to_all | solution.py:24
  86.3 10.6 %reduce-scatter.5.cloned.1.call-done = bf16[512,1024]{1,0:T(8,128)(2,1)} async-done(((bf16[2048,1024]{1,0:T(8,128)(2,1)}), bf16[512,1024]{1,0:T(8,128)(2,1)}) %reduce-scatter.5.cloned.1.call-update) | async-done | bytes 1048592 | tf_op jit(solution)/shard_map/reduce_scatter | solution.py:82
  96.9 2.3 convolution_convert_fusion.11
  99.2 2.1 convolution_convert_fusion.10
  101.3 2.1 convolution_convert_fusion.9
  103.4 2.1 convolution_convert_fusion.8
  105.6 1.0 pad_maximum_fusion.4
  106.6 5.1 %all-to-all-start.3 = ((bf16[8,256,256]{2,1,0:T(8,128)(2,1)}), bf16[8,256,256]{2,1,0:T(8,128)(2,1)S(1)}, u32[]{:S(2)}, u32[]{:S(2)}) async-start(bf16[8,256,256]{2,1,0:T(8,128)(2,1)} %bitcast.8), calls=%async_computation.4 | async-start | bytes 2097152 | tf_op jit(solution)/shard_map/all_to_all | solution.py:128
  111.8 54.4 %all-to-all-done.3 = bf16[8,256,256]{2,1,0:T(8,128)(2,1)S(1)} async-done(((bf16[8,256,256]{2,1,0:T(8,128)(2,1)}), bf16[8,256,256]{2,1,0:T(8,128)(2,1)S(1)}, u32[]{:S(2)}, u32[]{:S(2)}) %all-to-all-start.3) | async-done | bytes 1048608 | tf_op jit(solution)/shard_map/all_to_all | solution.py:128
  166.8 27.2 %reduce-scatter.7.cloned.1.call-done = bf16[512,1024]{1,0:T(8,128)(2,1)} async-done(((bf16[2048,1024]{1,0:T(8,128)(2,1)}), bf16[512,1024]{1,0:T(8,128)(2,1)}) %reduce-scatter.7.cloned.1.call-update) | async-done | bytes 1048592 | tf_op jit(solution)/shard_map/reduce_scatter | solution.py:82
  194.0 2.3 convolution_convert_fusion.4
  196.3 2.1 convolution_convert_fusion.5
  198.4 2.1 convolution_convert_fusion.6
  200.5 2.1 convolution_convert_fusion.7
  202.7 1.0 pad_maximum_fusion.5
  203.7 9.6 %all-to-all-start.4 = ((bf16[8,256,256]{2,1,0:T(8,128)(2,1)}), bf16[8,256,256]{2,1,0:T(8,128)(2,1)S(1)}, u32[]{:S(2)}, u32[]{:S(2)}) async-start(bf16[8,256,256]{2,1,0:T(8,128)(2,1)} %bitcast.10), calls=%async_computation.6 | async-start | bytes 2097152 | tf_op jit(solution)/shard_map/all_to_all | solution.py:128
  213.3 1.7 fusion.388
  215.0 1.5 pad_maximum_fusion.3
  216.6 50.7 %all-to-all-done.4 = bf16[8,256,256]{2,1,0:T(8,128)(2,1)S(1)} async-done(((bf16[8,256,256]{2,1,0:T(8,128)(2,1)}), bf16[8,256,256]{2,1,0:T(8,128)(2,1)S(1)}, u32[]{:S(2)}, u32[]{:S(2)}) %all-to-all-start.4) | async-done | bytes 1048608 | tf_op jit(solution)/shard_map/all_to_all | solution.py:128
  267.9 26.8 %reduce-scatter.9.cloned.1.call-done = bf16[512,1024]{1,0:T(8,128)(2,1)} async-done(((bf16[2048,1024]{1,0:T(8,128)(2,1)}), bf16[512,1024]{1,0:T(8,128)(2,1)}) %reduce-scatter.9.cloned.1.call-update) | async-done | bytes 1048592 | tf_op jit(solution)/shard_map/reduce_scatter | solution.py:82
  294.6 2.3 convolution_convert_fusion
  296.9 2.1 convolution_convert_fusion.1
  299.0 2.1 convolution_convert_fusion.2
  301.2 2.1 convolution_convert_fusion.3
  303.3 1.0 pad_maximum_fusion.6
  304.3 9.3 %all-to-all-start.5 = ((bf16[8,256,256]{2,1,0:T(8,128)(2,1)}), bf16[8,256,256]{2,1,0:T(8,128)(2,1)S(1)}, u32[]{:S(2)}, u32[]{:S(2)}) async-start(bf16[8,256,256]{2,1,0:T(8,128)(2,1)} %bitcast.12), calls=%async_computation.8 | async-start | bytes 2097152 | tf_op jit(solution)/shard_map/all_to_all | solution.py:128
  313.6 0.7 slice_dynamic-update-slice_fusion.3
  314.4 1.7 slice_dynamic-update-slice_fusion.11
  316.0 1.7 slice_dynamic-update-slice_fusion.7
  317.7 47.5 %all-to-all-done.5 = bf16[8,256,256]{2,1,0:T(8,128)(2,1)S(1)} async-done(((bf16[8,256,256]{2,1,0:T(8,128)(2,1)}), bf16[8,256,256]{2,1,0:T(8,128)(2,1)S(1)}, u32[]{:S(2)}, u32[]{:S(2)}) %all-to-all-start.5) | async-done | bytes 1048608 | tf_op jit(solution)/shard_map/all_to_all | solution.py:128
  365.8 1.7 slice_dynamic-update-slice_fusion.15
  367.5 0.7 slice_dynamic-update-slice_fusion.2
  368.2 1.7 slice_dynamic-update-slice_fusion.10
  369.9 1.7 slice_dynamic-update-slice_fusion.6
  371.5 1.6 slice_dynamic-update-slice_fusion.14
  373.1 0.7 slice_dynamic-update-slice_fusion.1
  373.8 1.7 slice_dynamic-update-slice_fusion.9
  375.5 1.7 slice_dynamic-update-slice_fusion.5
  377.2 0.7 slice_dynamic-update-slice_fusion.13
  377.9 1.6 convolution_convert_fusion.15
  379.5 1.7 convolution_convert_fusion.14
  381.1 1.6 convolution_convert_fusion.13
  382.8 1.7 convolution_convert_fusion.12
  384.4 0.8 pad_maximum_fusion.7
  385.3 5.2 %all-to-all-start.6 = ((bf16[8,256,128]{2,1,0:T(8,128)(2,1)}), bf16[8,256,128]{2,1,0:T(8,128)(2,1)S(1)}, u32[]{:S(2)}, u32[]{:S(2)}) async-start(bf16[8,256,128]{2,1,0:T(8,128)(2,1)} %bitcast.14), calls=%async_computation.10 | async-start | bytes 1048576 | tf_op jit(solution)/shard_map/all_to_all | solution.py:128
  390.5 0.7 slice_dynamic-update-slice_fusion
  391.2 1.7 slice_dynamic-update-slice_fusion.8
  392.9 1.7 slice_dynamic-update-slice_fusion.4
  394.6 0.7 slice_dynamic-update-slice_fusion.12
  395.2 9.8 %all-to-all-done.6 = bf16[8,256,128]{2,1,0:T(8,128)(2,1)S(1)} async-done(((bf16[8,256,128]{2,1,0:T(8,128)(2,1)}), bf16[8,256,128]{2,1,0:T(8,128)(2,1)S(1)}, u32[]{:S(2)}, u32[]{:S(2)}) %all-to-all-start.6) | async-done | bytes 524320 | tf_op jit(solution)/shard_map/all_to_all | solution.py:128
  405.4 0.7 broadcast_in_dim.48
  406.1 3.5 all-to-all-start.7
  409.6 17.6 %multiply_add_fusion = (f32[512,3584]{1,0:T(8,128)}, f32[512,3584]{1,0:T(8,128)}, bf16[512,3584]{1,0:T(8,128)(2,1)}, bf16[512,3584]{1,0:T(8,128)(2,1)}) fusion(f32[512,3584]{1,0:T(8,128)} %param.12, f32[512,3584]{1,0:T(8,128)} %param.9, bf16[512,3584]{1,0:T(8,128)(2,1)} %param.11, bf16[512,3584]{1,0:T(8,128)(2,1)} %slice_dynamic-update-slice_fusion.12, ...), kind=kLoop, calls=%fused_computation.5 | loop fusion | flops 38535168 | bytes 47710208 | tf_op jit(solution)/shard_map/add | solution.py:36
  427.2 0.6 reduce_sum.79
  (46 shorter events, 2.9 us)
Async XLA Ops:
  7.2 89.7 %reduce-scatter.5.cloned.1.call-start = ((), (), s32[]{:S(2)}) async-start(), calls=%async_computation.12 | async-start | bytes 5242880 | tf_op jit(solution)/shard_map/reduce_scatter | solution.py:82
  17.0 177.0 %reduce-scatter.7.cloned.1.call-start = ((), (), s32[]{:S(2)}) async-start(), calls=%async_computation.13 | async-start | bytes 5242880 | tf_op jit(solution)/shard_map/reduce_scatter | solution.py:82
  20.9 0.7 copy-start.5
  22.1 29.8 %all-to-all-start = ((s32[2,1,256]{2,1,0:T(1,128)}), s32[2,1,256]{2,1,0:T(1,128)S(1)}, u32[]{:S(2)}, u32[]{:S(2)}) async-start(s32[2,1,256]{2,1,0:T(1,128)} %broadcast_in_dim.23), calls=%async_computation.1 | async-start | bytes 4096 | tf_op jit(solution)/shard_map/all_to_all | solution.py:24
  26.3 268.3 %reduce-scatter.9.cloned.1.call-start = ((), (), s32[]{:S(2)}) async-start(), calls=%async_computation.14 | async-start | bytes 5242880 | tf_op jit(solution)/shard_map/reduce_scatter | solution.py:82
  96.9 2.3 copy-start
  103.4 8.3 %copy-start.6 = (s32[1,256]{1,0:T(1,128)S(1)}, s32[1,256]{1,0:T(1,128)}, u32[]{:S(2)}) copy-start(s32[1,256]{1,0:T(1,128)} %param.16) | copy-start | bytes 3076
  105.5 61.0 %copy-start.4 = (bf16[1,896,256]{2,1,0:T(8,128)(2,1)S(1)}, bf16[1,896,256]{2,1,0:T(8,128)(2,1)}, u32[]{:S(2)}) copy-start(bf16[1,896,256]{2,1,0:T(8,128)(2,1)} %param.17) | copy-start | bytes 1376260
  106.6 59.6 %all-to-all-start.3 = ((bf16[8,256,256]{2,1,0:T(8,128)(2,1)}), bf16[8,256,256]{2,1,0:T(8,128)(2,1)S(1)}, u32[]{:S(2)}, u32[]{:S(2)}) async-start(bf16[8,256,256]{2,1,0:T(8,128)(2,1)} %bitcast.8), calls=%async_computation.4 | async-start | bytes 2097152 | tf_op jit(solution)/shard_map/all_to_all | solution.py:128
  194.0 2.3 copy-start.1
  203.7 63.6 %all-to-all-start.4 = ((bf16[8,256,256]{2,1,0:T(8,128)(2,1)}), bf16[8,256,256]{2,1,0:T(8,128)(2,1)S(1)}, u32[]{:S(2)}, u32[]{:S(2)}) async-start(bf16[8,256,256]{2,1,0:T(8,128)(2,1)} %bitcast.10), calls=%async_computation.6 | async-start | bytes 2097152 | tf_op jit(solution)/shard_map/all_to_all | solution.py:128
  213.3 152.5 %reduce-scatter.11.cloned.1.call-start = ((), (), s32[]{:S(2)}) async-start(), calls=%async_computation.15 | async-start | bytes 2621440 | tf_op jit(solution)/shard_map/reduce_scatter | solution.py:82
  294.6 2.3 copy-start.2
  304.3 60.9 %all-to-all-start.5 = ((bf16[8,256,256]{2,1,0:T(8,128)(2,1)}), bf16[8,256,256]{2,1,0:T(8,128)(2,1)S(1)}, u32[]{:S(2)}, u32[]{:S(2)}) async-start(bf16[8,256,256]{2,1,0:T(8,128)(2,1)} %bitcast.12), calls=%async_computation.8 | async-start | bytes 2097152 | tf_op jit(solution)/shard_map/all_to_all | solution.py:128
  365.8 11.4 %copy-start.3 = (bf16[512,512]{1,0:T(8,128)(2,1)S(1)}, bf16[512,512]{1,0:T(8,128)(2,1)}, u32[]{:S(2)}) copy-start(bf16[512,512]{1,0:T(8,128)(2,1)} %reduce-scatter.11.cloned.1.call-done) | copy-start | bytes 1572868
  385.3 19.8 %all-to-all-start.6 = ((bf16[8,256,128]{2,1,0:T(8,128)(2,1)}), bf16[8,256,128]{2,1,0:T(8,128)(2,1)S(1)}, u32[]{:S(2)}, u32[]{:S(2)}) async-start(bf16[8,256,128]{2,1,0:T(8,128)(2,1)} %bitcast.14), calls=%async_computation.10 | async-start | bytes 1048576 | tf_op jit(solution)/shard_map/all_to_all | solution.py:128
  406.1 21.1 %all-to-all-start.7 = ((f32[16,8,256]{2,1,0:T(8,128)}), f32[16,8,256]{2,1,0:T(8,128)S(1)}, u32[]{:S(2)}, u32[]{:S(2)}) async-start(f32[16,8,256]{2,1,0:T(8,128)} %broadcast_in_dim.48), calls=%async_computation.11 | async-start | bytes 262144 | tf_op jit(solution)/shard_map/all_to_all | solution.py:24
Sparse Core Ops, SparseCore 0:
  17.1 79.7 reduce-scatter.4
  99.8 94.1 reduce-scatter.6
  196.3 98.2 reduce-scatter.8
  297.4 65.1 reduce-scatter.10
